TPU v7x, 32 devices: a whole 2x2x4 slice. The times are simulated.
32 devices in a mesh: gx: 8 (over z, x), gy: 4 (over y, core).
Axes of the slice: x: 2, y: 2, z: 4, core: 2. Of those that a mesh axis runs over, the one named last changes fastest.
Arguments:
- fields: float32 [5, 3, 1024, 2048], P(None, None, 'gx', 'gy'), may hold values from -6 to 6
- metric_first: float32 [1024], P('gx'), may hold values from 0.5 to 2
- metric_second: float32 [2048], P('gy'), may hold values from 0.5 to 2
Outputs:
- slope_first: float32 [5, 3, 1024, 2048], P(None, None, 'gx', 'gy')
- slope_second: float32 [5, 3, 1024, 2048], P(None, None, 'gx', 'gy')
All inputs are finite; a program needn't handle non-finite values.
Results may differ from a plain program's by a relative error of at most 0.00007.
Values sent between devices are 32-bit elements; how exact they have to be, the bound alone decides.
A program may use at most 128 MiB of HBM per device.

v0:
```python
import jax
import jax.numpy as jnp
from jax import lax
from jax.sharding import PartitionSpec as P

ALPHA = 0.47
COEF_A = 2.0 * (ALPHA + 2.0) / 3.0
COEF_B = (4.0 * ALPHA - 1.0) / 3.0
HIGHEST = lax.Precision.HIGHEST


def with_halo(cells, sides, width):
    for axis, dim in sides:
        count = lax.axis_size(axis)
        head = lax.slice_in_dim(cells, 0, width, axis=dim)
        tail = lax.slice_in_dim(cells, cells.shape[dim] - width, cells.shape[dim], axis=dim)
        cells = jnp.concatenate(
            [
                lax.ppermute(tail, axis, [(i, (i + 1) % count) for i in range(count)]),
                cells,
                lax.ppermute(head, axis, [((i + 1) % count, i) for i in range(count)]),
            ],
            axis=dim,
        )
    return cells


def from_behind(block, axis, distance):
    devices = range(lax.axis_size(axis))
    route = [((i - distance) % len(devices), i) for i in devices]
    return lax.ppermute(block, axis, route)


def explicit_side(padded, axis, extent):

    def shifted(offset):
        return lax.slice_in_dim(padded, 2 + offset, 2 + offset + extent, axis=axis)

    return COEF_A / 2.0 * (shifted(1) - shifted(-1)) + COEF_B / 4.0 * (shifted(2) - shifted(-2))


def line_inverse(extent):
    positions = jnp.arange(extent)
    diagonal = jnp.ones((extent,), jnp.float32)
    below_band = jnp.where(positions == 0, 0.0, ALPHA).astype(jnp.float32)
    above_band = jnp.where(positions == extent - 1, 0.0, ALPHA).astype(jnp.float32)
    return lax.linalg.tridiagonal_solve(
        below_band, diagonal, above_band, jnp.eye(extent, dtype=jnp.float32)
    )


def multiply_two(first_matrix, second_matrix):
    return jnp.matmul(first_matrix, second_matrix, precision=HIGHEST)


def invert_two(matrix):
    determinant = matrix[0, 0] * matrix[1, 1] - matrix[0, 1] * matrix[1, 0]
    adjugate = jnp.stack(
        [jnp.stack([matrix[1, 1], -matrix[0, 1]]), jnp.stack([-matrix[1, 0], matrix[0, 0]])]
    )
    return adjugate / determinant


def apply_two(matrix, values):
    return jnp.einsum("ij,j...->i...", matrix, values, precision=HIGHEST)


def reduced_blocks(inverse):
    zeroes = jnp.zeros((), jnp.float32)
    block_low = ALPHA * jnp.stack(
        [jnp.stack([zeroes, inverse[0, 0]]), jnp.stack([zeroes, inverse[-1, 0]])]
    )
    block_high = ALPHA * jnp.stack(
        [jnp.stack([inverse[0, -1], zeroes]), jnp.stack([inverse[-1, -1], zeroes])]
    )
    return (block_low, jnp.eye(2, dtype=jnp.float32), block_high)


def doubling(known, blocks, members, push):
    block_low, block_mid, block_high = blocks
    for section_number in range(members.bit_length() - 1):
        distance = 1 << section_number
        lower_term = push(known, distance)
        upper_term = push(known, -distance)
        inverse_mid = invert_two(block_mid)
        left_factor = multiply_two(block_low, inverse_mid)
        right_factor = multiply_two(block_high, inverse_mid)
        known = known - apply_two(left_factor, lower_term) - apply_two(right_factor, upper_term)
        block_mid = (
            block_mid
            - multiply_two(left_factor, block_high)
            - multiply_two(right_factor, block_low)
        )
        block_low = -multiply_two(left_factor, block_low)
        block_high = -multiply_two(right_factor, block_high)
    return apply_two(invert_two(block_low + block_mid + block_high), known)


def doubled(end_values, blocks, members, push):
    solved = doubling(end_values, blocks, members, push)
    return (push(solved[1], 1), push(solved[0], -1))


def piece_solve(force_first, force_second, reduce_first, reduce_second):
    inverse_first = line_inverse(force_first.shape[2])
    inverse_second = line_inverse(force_second.shape[3])
    local_first = jnp.einsum("ij,fpjk->fpik", inverse_first, force_first, precision=HIGHEST)
    local_second = jnp.einsum("fpkj,ij->fpki", force_second, inverse_second, precision=HIGHEST)
    ends_first = jnp.stack([local_first[:, :, 0, :], local_first[:, :, -1, :]])
    ends_second = jnp.stack([local_second[:, :, :, 0], local_second[:, :, :, -1]])
    left_value, right_value = reduce_first(ends_first, reduced_blocks(inverse_first))
    low_value, high_value = reduce_second(ends_second, reduced_blocks(inverse_second))
    compact_first = (
        local_first
        - ALPHA * left_value[:, :, None, :] * inverse_first[:, 0][:, None]
        - ALPHA * right_value[:, :, None, :] * inverse_first[:, -1][:, None]
    )
    compact_second = (
        local_second
        - ALPHA * low_value[..., None] * inverse_second[:, 0]
        - ALPHA * high_value[..., None] * inverse_second[:, -1]
    )
    return (compact_first, compact_second)


def shards(fields, metric_first, metric_second):
    extent_first = fields.shape[2]
    extent_second = fields.shape[3]
    width = 2
    padded = with_halo(fields, (("gx", 2), ("gy", 3)), width)
    force_first = explicit_side(padded[:, :, :, width:-width], 2, extent_first + 2 * width - 4)
    force_second = explicit_side(padded[:, :, width:-width, :], 3, extent_second + 2 * width - 4)
    compact_first, compact_second = piece_solve(
        force_first,
        force_second,
        lambda end_values, blocks: doubled(
            end_values,
            blocks,
            lax.axis_size("gx"),
            lambda values, distance: from_behind(values, "gx", distance),
        ),
        lambda end_values, blocks: doubled(
            end_values,
            blocks,
            lax.axis_size("gy"),
            lambda values, distance: from_behind(values, "gy", distance),
        ),
    )
    slope_first = metric_first[:, None] * compact_first
    slope_second = metric_second * compact_second
    return (slope_first, slope_second)


def solution(mesh):
    placed = (P(None, None, "gx", "gy"), P("gx"), P("gy"))
    return jax.shard_map(
        shards,
        mesh=mesh,
        in_specs=placed,
        out_specs=(P(None, None, "gx", "gy"), P(None, None, "gx", "gy")),
        check_vma=False,
    )
```

profile of v0, /device:TPU:0, one launch (start us, length us, event | category | flops | bytes accessed | tf_op | source)
XLA Modules:
  0.0 1933.1 jit_solution(7207592595754198023)
XLA Ops:
  11.5 978.3 %while.66 = (s32[]{:T(128)}, f32[]{:T(128)}, f32[512]{0:T(512)S(1)}, f32[15,32]{1,0:T(8,128)S(1)}, f32[15,32,512]{2,1,0:T(8,128)S(1)}, /*index=5*/f32[15,32]{1,0...) while((s32[]{:T(128)}, f32[]{:T(128)}, ...), condition=%wide.region_5.6_spmd, body=%wide.region_4.5_spmd.sunk | while | flops 49281 | bytes 534249 | solution.py:47
  1056.2 338.3 %while.67 = (s32[]{:T(128)}, f32[512]{0:T(512)S(1)}, f32[15,32,512]{2,1,0:T(8,128)S(1)}, f32[15,32,512]{2,1,0:T(8,128)S(1)}, f32[15,32]{1,0:T(8,128)}, /*index=5...) while((s32[]{:T(128)}, f32[512]{0:T(512)S(1)}, ...), condition=%wide.region_7.8_spmd, body=%wide.region_6.7_spmd.sunk | while | flops 32802 | bytes 531929 | solution.py:47
  1058.6 20.0 %multiply_subtract_fusion.125 = (f32[512]{0:T(512)S(1)}, f32[512]{0:T(512)S(1)}, f32[512]{0:T(512)S(1)}, f32[512]{0:T(512)S(1)}, f32[512]{0:T(512)S(1)}, /*index...) fusion(f32[512]{0:T(512)S(1)} %bitcast.2965, ...), kind=kLoop, calls=%fused_computation.330.clone.1 | loop fusion | flops 32768 | bytes 133248 | tf_op jit(solution)/shard_map/while/body/eval_jaxpr/sub | solution.py:47
  1081.1 20.0 %multiply_subtract_fusion.125 = (f32[512]{0:T(512)S(1)}, f32[512]{0:T(512)S(1)}, f32[512]{0:T(512)S(1)}, f32[512]{0:T(512)S(1)}, f32[512]{0:T(512)S(1)}, /*index...) fusion(f32[512]{0:T(512)S(1)} %bitcast.2965, ...), kind=kLoop, calls=%fused_computation.330.clone.1 | loop fusion | flops 32768 | bytes 133248 | tf_op jit(solution)/shard_map/while/body/eval_jaxpr/sub | solution.py:47
  1103.7 20.0 %multiply_subtract_fusion.125 = (f32[512]{0:T(512)S(1)}, f32[512]{0:T(512)S(1)}, f32[512]{0:T(512)S(1)}, f32[512]{0:T(512)S(1)}, f32[512]{0:T(512)S(1)}, /*index...) fusion(f32[512]{0:T(512)S(1)} %bitcast.2965, ...), kind=kLoop, calls=%fused_computation.330.clone.1 | loop fusion | flops 32768 | bytes 133248 | tf_op jit(solution)/shard_map/while/body/eval_jaxpr/sub | solution.py:47
  1126.2 20.0 %multiply_subtract_fusion.125 = (f32[512]{0:T(512)S(1)}, f32[512]{0:T(512)S(1)}, f32[512]{0:T(512)S(1)}, f32[512]{0:T(512)S(1)}, f32[512]{0:T(512)S(1)}, /*index...) fusion(f32[512]{0:T(512)S(1)} %bitcast.2965, ...), kind=kLoop, calls=%fused_computation.330.clone.1 | loop fusion | flops 32768 | bytes 133248 | tf_op jit(solution)/shard_map/while/body/eval_jaxpr/sub | solution.py:47
  1148.8 20.0 %multiply_subtract_fusion.125 = (f32[512]{0:T(512)S(1)}, f32[512]{0:T(512)S(1)}, f32[512]{0:T(512)S(1)}, f32[512]{0:T(512)S(1)}, f32[512]{0:T(512)S(1)}, /*index...) fusion(f32[512]{0:T(512)S(1)} %bitcast.2965, ...), kind=kLoop, calls=%fused_computation.330.clone.1 | loop fusion | flops 32768 | bytes 133248 | tf_op jit(solution)/shard_map/while/body/eval_jaxpr/sub | solution.py:47
  1171.3 20.0 %multiply_subtract_fusion.125 = (f32[512]{0:T(512)S(1)}, f32[512]{0:T(512)S(1)}, f32[512]{0:T(512)S(1)}, f32[512]{0:T(512)S(1)}, f32[512]{0:T(512)S(1)}, /*index...) fusion(f32[512]{0:T(512)S(1)} %bitcast.2965, ...), kind=kLoop, calls=%fused_computation.330.clone.1 | loop fusion | flops 32768 | bytes 133248 | tf_op jit(solution)/shard_map/while/body/eval_jaxpr/sub | solution.py:47
  1193.9 20.0 %multiply_subtract_fusion.125 = (f32[512]{0:T(512)S(1)}, f32[512]{0:T(512)S(1)}, f32[512]{0:T(512)S(1)}, f32[512]{0:T(512)S(1)}, f32[512]{0:T(512)S(1)}, /*index...) fusion(f32[512]{0:T(512)S(1)} %bitcast.2965, ...), kind=kLoop, calls=%fused_computation.330.clone.1 | loop fusion | flops 32768 | bytes 133248 | tf_op jit(solution)/shard_map/while/body/eval_jaxpr/sub | solution.py:47
  1216.4 20.0 %multiply_subtract_fusion.125 = (f32[512]{0:T(512)S(1)}, f32[512]{0:T(512)S(1)}, f32[512]{0:T(512)S(1)}, f32[512]{0:T(512)S(1)}, f32[512]{0:T(512)S(1)}, /*index...) fusion(f32[512]{0:T(512)S(1)} %bitcast.2965, ...), kind=kLoop, calls=%fused_computation.330.clone.1 | loop fusion | flops 32768 | bytes 133248 | tf_op jit(solution)/shard_map/while/body/eval_jaxpr/sub | solution.py:47
  1239.0 20.0 %multiply_subtract_fusion.125 = (f32[512]{0:T(512)S(1)}, f32[512]{0:T(512)S(1)}, f32[512]{0:T(512)S(1)}, f32[512]{0:T(512)S(1)}, f32[512]{0:T(512)S(1)}, /*index...) fusion(f32[512]{0:T(512)S(1)} %bitcast.2965, ...), kind=kLoop, calls=%fused_computation.330.clone.1 | loop fusion | flops 32768 | bytes 133248 | tf_op jit(solution)/shard_map/while/body/eval_jaxpr/sub | solution.py:47
  1261.6 20.0 %multiply_subtract_fusion.125 = (f32[512]{0:T(512)S(1)}, f32[512]{0:T(512)S(1)}, f32[512]{0:T(512)S(1)}, f32[512]{0:T(512)S(1)}, f32[512]{0:T(512)S(1)}, /*index...) fusion(f32[512]{0:T(512)S(1)} %bitcast.2965, ...), kind=kLoop, calls=%fused_computation.330.clone.1 | loop fusion | flops 32768 | bytes 133248 | tf_op jit(solution)/shard_map/while/body/eval_jaxpr/sub | solution.py:47
  1284.1 20.0 %multiply_subtract_fusion.125 = (f32[512]{0:T(512)S(1)}, f32[512]{0:T(512)S(1)}, f32[512]{0:T(512)S(1)}, f32[512]{0:T(512)S(1)}, f32[512]{0:T(512)S(1)}, /*index...) fusion(f32[512]{0:T(512)S(1)} %bitcast.2965, ...), kind=kLoop, calls=%fused_computation.330.clone.1 | loop fusion | flops 32768 | bytes 133248 | tf_op jit(solution)/shard_map/while/body/eval_jaxpr/sub | solution.py:47
  1306.7 20.0 %multiply_subtract_fusion.125 = (f32[512]{0:T(512)S(1)}, f32[512]{0:T(512)S(1)}, f32[512]{0:T(512)S(1)}, f32[512]{0:T(512)S(1)}, f32[512]{0:T(512)S(1)}, /*index...) fusion(f32[512]{0:T(512)S(1)} %bitcast.2965, ...), kind=kLoop, calls=%fused_computation.330.clone.1 | loop fusion | flops 32768 | bytes 133248 | tf_op jit(solution)/shard_map/while/body/eval_jaxpr/sub | solution.py:47
  1329.2 20.0 %multiply_subtract_fusion.125 = (f32[512]{0:T(512)S(1)}, f32[512]{0:T(512)S(1)}, f32[512]{0:T(512)S(1)}, f32[512]{0:T(512)S(1)}, f32[512]{0:T(512)S(1)}, /*index...) fusion(f32[512]{0:T(512)S(1)} %bitcast.2965, ...), kind=kLoop, calls=%fused_computation.330.clone.1 | loop fusion | flops 32768 | bytes 133248 | tf_op jit(solution)/shard_map/while/body/eval_jaxpr/sub | solution.py:47
  1351.8 20.0 %multiply_subtract_fusion.125 = (f32[512]{0:T(512)S(1)}, f32[512]{0:T(512)S(1)}, f32[512]{0:T(512)S(1)}, f32[512]{0:T(512)S(1)}, f32[512]{0:T(512)S(1)}, /*index...) fusion(f32[512]{0:T(512)S(1)} %bitcast.2965, ...), kind=kLoop, calls=%fused_computation.330.clone.1 | loop fusion | flops 32768 | bytes 133248 | tf_op jit(solution)/shard_map/while/body/eval_jaxpr/sub | solution.py:47
  1440.3 195.8 %while.64 = (s32[]{:T(128)}, f32[]{:T(128)}, f32[128]{0:T(128)S(1)}, f32[3,32]{1,0:T(4,128)S(1)}, f32[3,32,128]{2,1,0:T(8,128)S(1)}, /*index=5*/f32[3,32]{1,0:T(...) while((s32[]{:T(128)}, f32[]{:T(128)}, ...), condition=%wide.region_1.2_spmd, body=%wide.region_0.1_spmd.sunk | while | flops 12417 | bytes 103653 | solution.py:47
  1483.5 20.0 %fusion.592 = (f32[128]{0:T(128)S(1)}, f32[128]{0:T(128)S(1)}, f32[128]{0:T(128)S(1)}, f32[128]{0:T(128)S(1)}, f32[128]{0:T(128)S(1)}, /*index=5*/f32[128]{0:T(1...) fusion(f32[3,32,128]{2,1,0:T(8,128)S(1)} %get-tuple-element.220, ...), kind=kLoop, calls=%fused_computation.40.clone.1 | loop fusion | flops 12288 | bytes 33664 | tf_op jit(solution)/shard_map/while/body/eval_jaxpr/div | solution.py:47
  1548.7 20.0 %fusion.592 = (f32[128]{0:T(128)S(1)}, f32[128]{0:T(128)S(1)}, f32[128]{0:T(128)S(1)}, f32[128]{0:T(128)S(1)}, f32[128]{0:T(128)S(1)}, /*index=5*/f32[128]{0:T(1...) fusion(f32[3,32,128]{2,1,0:T(8,128)S(1)} %get-tuple-element.220, ...), kind=kLoop, calls=%fused_computation.40.clone.1 | loop fusion | flops 12288 | bytes 33664 | tf_op jit(solution)/shard_map/while/body/eval_jaxpr/div | solution.py:47
  1614.0 20.0 %fusion.592 = (f32[128]{0:T(128)S(1)}, f32[128]{0:T(128)S(1)}, f32[128]{0:T(128)S(1)}, f32[128]{0:T(128)S(1)}, f32[128]{0:T(128)S(1)}, /*index=5*/f32[128]{0:T(1...) fusion(f32[3,32,128]{2,1,0:T(8,128)S(1)} %get-tuple-element.220, ...), kind=kLoop, calls=%fused_computation.40.clone.1 | loop fusion | flops 12288 | bytes 33664 | tf_op jit(solution)/shard_map/while/body/eval_jaxpr/div | solution.py:47
  1696.6 65.0 %while.65 = (s32[]{:T(128)}, f32[128]{0:T(128)S(1)}, f32[3,32,128]{2,1,0:T(8,128)S(1)}, f32[3,32,128]{2,1,0:T(8,128)S(1)}, f32[3,32]{1,0:T(4,128)S(1)}, /*index=...) while((s32[]{:T(128)}, f32[128]{0:T(128)S(1)}, ...), condition=%wide.region_3.4_spmd, body=%wide.region_2.3_spmd.sunk | while | flops 8226 | bytes 101333 | solution.py:47
  1698.0 20.1 %fusion.595 = (f32[128]{0:T(128)S(1)}, f32[128]{0:T(128)S(1)}, f32[128]{0:T(128)S(1)}, f32[128]{0:T(128)S(1)}, f32[128]{0:T(128)S(1)}, /*index=5*/f32[128]{0:T(1...) fusion(f32[3,32,128]{2,1,0:T(8,128)S(1)} %get-tuple-element.232, ...), kind=kLoop, calls=%fused_computation.168.clone.1 | loop fusion | flops 8192 | bytes 33536 | tf_op jit(solution)/shard_map/while/body/eval_jaxpr/sub | solution.py:47
  1719.7 20.1 %fusion.595 = (f32[128]{0:T(128)S(1)}, f32[128]{0:T(128)S(1)}, f32[128]{0:T(128)S(1)}, f32[128]{0:T(128)S(1)}, f32[128]{0:T(128)S(1)}, /*index=5*/f32[128]{0:T(1...) fusion(f32[3,32,128]{2,1,0:T(8,128)S(1)} %get-tuple-element.232, ...), kind=kLoop, calls=%fused_computation.168.clone.1 | loop fusion | flops 8192 | bytes 33536 | tf_op jit(solution)/shard_map/while/body/eval_jaxpr/sub | solution.py:47
  1741.4 20.1 %fusion.595 = (f32[128]{0:T(128)S(1)}, f32[128]{0:T(128)S(1)}, f32[128]{0:T(128)S(1)}, f32[128]{0:T(128)S(1)}, f32[128]{0:T(128)S(1)}, /*index=5*/f32[128]{0:T(1...) fusion(f32[3,32,128]{2,1,0:T(8,128)S(1)} %get-tuple-element.232, ...), kind=kLoop, calls=%fused_computation.168.clone.1 | loop fusion | flops 8192 | bytes 33536 | tf_op jit(solution)/shard_map/while/body/eval_jaxpr/sub | solution.py:47
  (614 shorter events, 685.5 us)
Async XLA Ops:
  1.8 1833.2 %collective-permute-start.1 = (f32[5,3,2,512]{3,0,2,1:T(8,128)S(1)}, f32[5,3,2,512]{3,0,2,1:T(8,128)S(1)}, u32[]{:S(2)}, u32[]{:S(2)}) collective-permute-start(f32[5,3,2,512]{3,0,2,1:T(8,128)S(1)} %copy.74), channel_id=1, source_target_pairs={{0,4},{4,8},{8,12},{12,16},{16,20},{20,24},{24,28},{28,0},{1,5},{5... | collective-permute-start | bytes 184328 | tf_op jit(solution)/shard_map/ppermute | solution.py:19
  4.8 1834.2 %collective-permute-start = (f32[5,3,2,512]{3,0,2,1:T(8,128)S(1)}, f32[5,3,2,512]{3,0,2,1:T(8,128)S(1)}, u32[]{:S(2)}, u32[]{:S(2)}) collective-permute-start(f32[5,3,2,512]{3,0,2,1:T(8,128)S(1)} %copy.73), channel_id=1, source_target_pairs={{4,0},{8,4},{12,8},{16,12},{20,16},{24,20},{28,24},{0,28},{5,1},{9... | collective-permute-start | bytes 184328 | tf_op jit(solution)/shard_map/ppermute | solution.py:21
  1056.0 338.6 %copy-start.5 = (f32[1,512]{1,0:T(1,128)S(1)}, f32[1,512]{1,0:T(1,128)}, u32[]{:S(2)}) copy-start(f32[1,512]{1,0:T(1,128)} %get-tuple-element.940) | copy-start | bytes 6148
  1056.0 338.5 %copy-start.6 = (f32[1,512]{1,0:T(1,128)S(1)}, f32[1,512]{1,0:T(1,128)}, u32[]{:S(2)}) copy-start(f32[1,512]{1,0:T(1,128)} %get-tuple-element.941) | copy-start | bytes 6148
  1056.0 338.5 %copy-start.7 = (f32[1,512]{1,0:T(1,128)S(1)}, f32[1,512]{1,0:T(1,128)}, u32[]{:S(2)}) copy-start(f32[1,512]{1,0:T(1,128)} %get-tuple-element.942) | copy-start | bytes 6148
  1056.0 338.5 %copy-start.8 = (f32[1,512]{1,0:T(1,128)S(1)}, f32[1,512]{1,0:T(1,128)}, u32[]{:S(2)}) copy-start(f32[1,512]{1,0:T(1,128)} %get-tuple-element.943) | copy-start | bytes 6148
  1056.0 338.5 %copy-start.9 = (f32[1,512]{1,0:T(1,128)S(1)}, f32[1,512]{1,0:T(1,128)}, u32[]{:S(2)}) copy-start(f32[1,512]{1,0:T(1,128)} %get-tuple-element.944) | copy-start | bytes 6148
  1056.0 338.5 %copy-start.10 = (f32[1,512]{1,0:T(1,128)S(1)}, f32[1,512]{1,0:T(1,128)}, u32[]{:S(2)}) copy-start(f32[1,512]{1,0:T(1,128)} %get-tuple-element.945) | copy-start | bytes 6148
  1056.0 338.5 %copy-start.11 = (f32[1,512]{1,0:T(1,128)S(1)}, f32[1,512]{1,0:T(1,128)}, u32[]{:S(2)}) copy-start(f32[1,512]{1,0:T(1,128)} %get-tuple-element.946) | copy-start | bytes 6148
  1056.1 338.5 %copy-start.12 = (f32[1,512]{1,0:T(1,128)S(1)}, f32[1,512]{1,0:T(1,128)}, u32[]{:S(2)}) copy-start(f32[1,512]{1,0:T(1,128)} %get-tuple-element.947) | copy-start | bytes 6148
  1858.2 17.0 collective-permute-start.9
  1858.9 16.6 collective-permute-start.10
  1891.3 3.2 collective-permute-start.12
  1893.2 3.2 collective-permute-start.11
  1896.6 3.8 collective-permute-start.13
  1897.8 4.3 collective-permute-start.3
  1899.6 6.9 collective-permute-start.2
  1901.0 6.0 collective-permute-start.15
  1901.1 13.0 collective-permute-start.14
  1906.9 4.3 collective-permute-start.5
  1907.0 6.7 collective-permute-start.4
  1914.0 6.0 collective-permute-start.6
  1921.1 4.5 collective-permute-start.8
  1923.6 6.8 collective-permute-start.7
  (11 other events, 1574.7 us)
where the time goes:
time: 1960 us; the launch traced here: 1930 us
  other arithmetic  848 us (43%)
  loops' own time  745 us (38%)
  local copies, waits for them, and re-layouts  170 us (9%)
  between operations  102 us (5%)
  matrix products  28.6 us (1%)
  waiting for transfers between devices  22.7 us (1%)
    another operation x4, loops' own time, line_inverse(): lax.linalg.tridiagonal_solve(below_band, diagonal, above_band, jnp.eye(ex...  745 us
    div x20, other arithmetic, line_inverse(): lax.linalg.tridiagonal_solve(below_band, diagonal, above_band, jnp.eye(ex...  397 us
    sub x19, other arithmetic, line_inverse(): lax.linalg.tridiagonal_solve(below_band, diagonal, above_band, jnp.eye(ex...  380 us
    slice x194, local copies, waits for them, and re-layouts, line_inverse(): lax.linalg.tridiagonal_solve(below_band, diagonal, above_band, jnp.eye(ex...  92.6 us
    broadcast_in_dim x18, other arithmetic, line_inverse(): lax.linalg.tridiagonal_solve(below_band, diagonal, above_band, jnp.eye(ex...  40.8 us
  transfers between devices with their start and end apart: 16, of which 9 were waited for; matrix products, arithmetic and copies ran while one was open for 52% of the time, Pallas kernels for 0%

commit v1 on v0

v1 whole, which is shorter than its diff:
```python
import jax
import jax.numpy as jnp
import ml_dtypes
import numpy as np
from jax import lax
from jax.experimental import pallas as pl
from jax.experimental.pallas import tpu as pltpu
from jax.sharding import PartitionSpec as P

ALPHA = 0.47
HALF_A = (ALPHA + 2.0) / 3.0
QUARTER_B = (4.0 * ALPHA - 1.0) / 12.0

ROOT = (-1.0 + np.sqrt(1.0 - 4.0 * ALPHA * ALPHA)) / (2.0 * ALPHA)
GAIN = 1.0 / (1.0 + 2.0 * ALPHA * ROOT)
KAPPA = GAIN * (HALF_A * (ROOT - 1.0 / ROOT) + QUARTER_B * (ROOT**2 - ROOT**-2))
DELTA = GAIN * QUARTER_B * (1.0 / ROOT - ROOT)

HIGHEST = lax.Precision.HIGHEST
MIB = 1 << 20


def piece_matrix(extent):
    place = np.arange(extent)
    gap = place[:, None] - place[None, :]
    size = np.abs(gap)
    whole = np.sign(gap) * (KAPPA * ROOT**size + np.where(size == 1, DELTA, 0.0))
    high = whole.astype(ml_dtypes.bfloat16)
    low = (whole - high.astype(np.float64)).astype(ml_dtypes.bfloat16)
    return high, low


def sum_weights(extent):
    place = np.arange(extent)
    rows = np.zeros((8, extent))
    rows[0] = ROOT ** (extent - place)
    rows[1] = ROOT ** (place + 1)
    rows[2, -1] = 1.0
    rows[3, 0] = 1.0
    return rows.astype(np.float32)


def edge_profiles(extent, members):
    place = np.arange(extent)
    whole_turn = 1.0 - ROOT ** (extent * members)
    rows = np.zeros((8, extent))
    rows[0] = KAPPA * ROOT**place / whole_turn
    rows[1] = -KAPPA * ROOT ** (extent - 1 - place) / whole_turn
    rows[2, 0] = DELTA
    rows[3, -1] = -DELTA
    return rows.astype(np.float32)


def split(values):
    high = values.astype(jnp.bfloat16)
    return high, (values - high.astype(jnp.float32)).astype(jnp.bfloat16)


def dot(left, right):
    return jnp.dot(left, right, preferred_element_type=jnp.float32)


def sums_kernel(u_ref, wx_ref, wy_ref, pair_ref, upper_ref, lower_ref, side_ref):
    step = pl.program_id(0)
    for plane in range(u_ref.shape[1]):
        u = u_ref[0, plane]
        slab = step * u_ref.shape[1] + plane
        along_x = jnp.dot(wx_ref[...], u, precision=HIGHEST, preferred_element_type=jnp.float32)
        for k in range(2):
            for target in (pair_ref, upper_ref, lower_ref):
                target[k, pl.ds(slab, 1), :] = along_x[k : k + 1]
        upper_ref[2, pl.ds(slab, 1), :] = along_x[2:3]
        lower_ref[2, pl.ds(slab, 1), :] = along_x[3:4]
        side_ref[0, plane] = lax.dot_general(
            wy_ref[...], u, (((1,), (1,)), ((), ())),
            precision=HIGHEST, preferred_element_type=jnp.float32,
        )


def second_kernel(u_ref, edge_ref, high_ref, low_ref, profile_ref, metric_ref, out_ref):
    planes, rows, columns = u_ref.shape[1:]
    u = u_ref[0].reshape(planes * rows, columns)
    u_high, u_low = split(u)
    total = dot(u_high, high_ref[...]) + dot(u_low, high_ref[...]) + dot(u_high, low_ref[...])
    metric = metric_ref[...]
    for plane in range(planes):
        edge = edge_ref[0, plane].T
        piece = total[plane * rows : (plane + 1) * rows]
        for k in range(4):
            piece = piece + edge[:, k : k + 1] * profile_ref[k : k + 1, :]
        out_ref[0, plane] = piece * metric


def first_kernel(u_ref, edge_ref, high_ref, low_ref, profile_ref, metric_ref, out_ref):
    planes = u_ref.shape[1]
    step = pl.program_id(0)
    left = jnp.concatenate([high_ref[...], high_ref[...], low_ref[...]], axis=1)
    metric = metric_ref[...]
    for plane in range(planes):
        u_high, u_low = split(u_ref[0, plane])
        total = dot(left, jnp.concatenate([u_high, u_low, u_high], axis=0))
        slab = step * planes + plane
        for k in range(4):
            total = total + profile_ref[:, k : k + 1] * edge_ref[k, pl.ds(slab, 1), :]
        out_ref[0, plane] = total * metric


def moved(block, axis, distance):
    count = lax.axis_size(axis)
    return lax.ppermute(block, axis, [(i, (i + distance) % count) for i in range(count)])


def whole(shape):
    return pl.BlockSpec(shape, lambda f: (0,) * len(shape))


def shards(fields, metric_first, metric_second):
    count, planes, rows, columns = fields.shape
    slabs = count * planes
    gx, gy = lax.axis_size("gx"), lax.axis_size("gy")
    slab_spec = pl.BlockSpec((1, planes, rows, columns), lambda f: (f, 0, 0, 0))
    params = pltpu.CompilerParams(vmem_limit_bytes=40 * MIB)
    size = fields.size
    shape = jax.ShapeDtypeStruct
    f32 = jnp.float32

    pair, upper, lower, side = pl.pallas_call(
        sums_kernel,
        grid=(count,),
        in_specs=[slab_spec, whole((8, rows)), whole((8, columns))],
        out_specs=[
            whole((2, slabs, columns)),
            whole((3, slabs, columns)),
            whole((3, slabs, columns)),
            pl.BlockSpec((1, planes, 8, rows), lambda f: (f, 0, 0, 0)),
        ],
        out_shape=[
            shape((2, slabs, columns), f32),
            shape((3, slabs, columns), f32),
            shape((3, slabs, columns), f32),
            shape((count, planes, 8, rows), f32),
        ],
        compiler_params=params,
        cost_estimate=pl.CostEstimate(flops=32 * size, bytes_accessed=4 * size, transcendentals=0),
    )(fields, sum_weights(rows), sum_weights(columns))

    sides = [moved(side[:, :, :4], "gy", q) for q in range(1, gy)] + [side[:, :, :4]]
    up = moved(upper, "gx", 1)
    down = moved(lower, "gx", -1)
    pairs = [up] + [moved(pair, "gx", q) for q in range(2, gx - 1)] + [down, pair]

    factor = np.float32(ROOT**columns)
    below, above = sides[gy - 1][:, :, 0], sides[gy - 1][:, :, 1]
    for q in range(gy - 1, 0, -1):
        below = sides[q - 1][:, :, 0] + factor * below
        above = sides[gy - q - 1][:, :, 1] + factor * above
    blank = jnp.zeros_like(below)
    edge_second = jnp.stack(
        [below, above, sides[0][:, :, 2], sides[gy - 2][:, :, 3]] + [blank] * 4, axis=2
    )

    high, low = piece_matrix(columns)
    slope_second = pl.pallas_call(
        second_kernel,
        grid=(count,),
        in_specs=[
            slab_spec,
            pl.BlockSpec((1, planes, 8, rows), lambda f: (f, 0, 0, 0)),
            whole((columns, columns)),
            whole((columns, columns)),
            whole((8, columns)),
            whole((1, columns)),
        ],
        out_specs=slab_spec,
        out_shape=shape(fields.shape, f32),
        compiler_params=params,
        cost_estimate=pl.CostEstimate(
            flops=6 * size * columns, bytes_accessed=8 * size, transcendentals=0
        ),
    )(
        fields, edge_second, np.ascontiguousarray(high.T), np.ascontiguousarray(low.T),
        edge_profiles(columns, gy), metric_second[None, :],
    )

    factor = np.float32(ROOT**rows)
    below, above = pairs[gx - 1][0], pairs[gx - 1][1]
    for q in range(gx - 1, 0, -1):
        below = pairs[q - 1][0] + factor * below
        above = pairs[gx - q - 1][1] + factor * above
    edge_first = jnp.stack([below, above, up[2], down[2]])

    high, low = piece_matrix(rows)
    slope_first = pl.pallas_call(
        first_kernel,
        grid=(count,),
        in_specs=[
            slab_spec,
            whole((4, slabs, columns)),
            whole((rows, rows)),
            whole((rows, rows)),
            whole((rows, 8)),
            whole((rows, 1)),
        ],
        out_specs=slab_spec,
        out_shape=shape(fields.shape, f32),
        compiler_params=params,
        cost_estimate=pl.CostEstimate(
            flops=6 * size * rows, bytes_accessed=8 * size, transcendentals=0
        ),
    )(
        fields, edge_first, high, low,
        np.ascontiguousarray(edge_profiles(rows, gx).T), metric_first[:, None],
    )
    return slope_first, slope_second


def solution(mesh):
    placed = (P(None, None, "gx", "gy"), P("gx"), P("gy"))
    return jax.shard_map(
        shards,
        mesh=mesh,
        in_specs=placed,
        out_specs=(P(None, None, "gx", "gy"), P(None, None, "gx", "gy")),
        check_vma=False,
    )
```

time: 1960 us -> 40.9 us (0.02); the launches traced: 1930 us -> 40.6 us
  other arithmetic: 848 us -> 0.12 us
  loops' own time: 745 us -> 0 us
  local copies, waits for them, and re-layouts: 170 us -> 5.85 us
  between operations: 102 us -> 0.76 us
  matrix products: 28.6 us -> 0 us
  waiting for transfers between devices: 22.7 us -> 0.03 us
    another operation x4 -> x0, loops' own time: 745 us -> none  [line_inverse(): lax.linalg.tridiagonal_solve(below_band, diagonal, above_band, jnp.eye(ex...]
    div x24 -> x0, other arithmetic: 397 us -> none  [the longest x20 397 us: line_inverse(): lax.linalg.tridiagonal_solve(below_band, diagonal, above_band, jnp.eye(ex...]
    sub x19 -> x0, other arithmetic: 380 us -> none  [line_inverse(): lax.linalg.tridiagonal_solve(below_band, diagonal, above_band, jnp.eye(ex...]
    slice x211 -> x1, local copies, waits for them, and re-layouts: 102 us -> 0.01 us  [shards(): side[:, :, :4]]
    broadcast_in_dim x18 -> x0, other arithmetic: 40.8 us -> none  [line_inverse(): lax.linalg.tridiagonal_solve(below_band, diagonal, above_band, jnp.eye(ex...]
    concatenate x62 -> x0, local copies, waits for them, and re-layouts: 31.2 us -> none  [the longest x60 21.8 us: line_inverse(): lax.linalg.tridiagonal_solve(below_band, diagonal, above_band, jnp.eye(ex...]
    dot_general x44 -> x0, matrix products: 28.6 us -> none  [the longest x1 14.4 us: piece_solve(): jnp.einsum('fpkj,ij->fpki', force_second, inverse_second, precision=HIGHEST)]
    ppermute x16 -> x10, waiting for transfers between devices: 22.7 us -> 0.03 us  [moved(): lax.ppermute(block, axis, [(i, (i + distance) % count) for i in range(cou...]
  transfers between devices with their start and end apart: 16 -> 10, of which waited for: 9 -> 0; matrix products, arithmetic and copies ran while one was open for 52% -> 1% of each run, Pallas kernels for 0% -> 14%
where the time goes in v1:
time: 40.9 us; the launch traced here: 40.6 us
  starting transfers between devices  18.5 us (45%)
  Pallas kernels  15.4 us (38%)
  local copies, waits for them, and re-layouts  5.85 us (14%)
  between operations  0.76 us (2%)
    ppermute x10, starting transfers between devices, moved(): lax.ppermute(block, axis, [(i, (i + distance) % count) for i in range(cou...  18.5 us
    pallas_call x1, Pallas kernels, shards(): pl.pallas_call(second_kernel, grid=(count,), in_specs=[slab_spec, pl.Bloc...  5.66 us
    unnamed x24, local copies, waits for them, and re-layouts  5.65 us
    pallas_call x1, Pallas kernels, shards(): pl.pallas_call(sums_kernel, grid=(count,), in_specs=[slab_spec, whole((8,...  5.52 us
    pallas_call x1, Pallas kernels, shards(): pl.pallas_call(first_kernel, grid=(count,), in_specs=[slab_spec, whole((4...  4.16 us
  transfers between devices with their start and end apart: 10, of which 0 were waited for; matrix products, arithmetic and copies ran while one was open for 1% of the time, Pallas kernels for 14%

profile of v1, /device:TPU:0, one launch (start us, length us, event | category | flops | bytes accessed | tf_op | source)
XLA Modules:
  0.0 40.6 jit_solution(15045534323673720472)
XLA Ops:
  0.6 0.0 copy-start
  0.6 2.1 %copy-done = f32[5,3,128,512]{3,2,1,0:T(8,128)S(1)} copy-done((f32[5,3,128,512]{3,2,1,0:T(8,128)S(1)}, f32[5,3,128,512]{3,2,1,0:T(8,128)}, u32[]{:S(2)}) %copy-start) | copy-done | bytes 3932184
  2.7 0.7 %copy-done.5 = f32[8,512]{1,0:T(8,128)S(1)} copy-done((f32[8,512]{1,0:T(8,128)S(1)}, f32[8,512]{1,0:T(8,128)}, u32[]{:S(2)}) %copy-start.5) | copy-done | bytes 16408
  3.5 0.7 %copy-done.6 = f32[8,128]{1,0:T(8,128)S(1)} copy-done((f32[8,128]{1,0:T(8,128)S(1)}, f32[8,128]{1,0:T(8,128)}, u32[]{:S(2)}) %copy-start.6) | copy-done | bytes 4120
  4.2 0.0 copy-start.10
  4.2 5.5 %shard_map.122 = (f32[2,15,512]{2,1,0:T(8,128)S(1)}, f32[3,15,512]{2,1,0:T(8,128)S(1)}, f32[3,15,512]{2,1,0:T(8,128)S(1)}, f32[5,3,8,128]{3,2,1,0:T(8,128)S(1)}) custom-call(f32[5,3,128,512]{3,2,1,0:T(8,128)S(1)} %copy-done, f32[8,128]{1,0:T(8,128)S(1)} %copy-done.6, f32[8,512]{1,0:T(8,128)S(1)} %copy-done.5), custom_call_target="tpu_custom_call" | custom-call | flops 31457280 | bytes 3932160 | tf_op jit(solution)/shard_map/pallas_call | solution.py:127
  9.7 2.4 %collective-permute-start.9 = (f32[5,3,4,128]{3,2,1,0:T(4,128)S(1)}, f32[5,3,4,128]{3,2,1,0:T(4,128)S(1)}, u32[]{:S(2)}, u32[]{:S(2)}) collective-permute-start(f32[5,3,4,128]{3,2,1,0:T(4,128)S(1)} %slice.110), channel_id=1, source_target_pairs={{0,3},{1,0},{2,1},{3,2},{4,7},{5,4},{6,5},{7,6},{8,11},{9,8},{10,9... | collective-permute-start | bytes 92168 | tf_op jit(solution)/shard_map/ppermute | solution.py:110
  12.1 0.6 %collective-permute-start.8 = (f32[5,3,4,128]{3,2,1,0:T(4,128)S(1)}, f32[5,3,4,128]{3,2,1,0:T(4,128)S(1)}, u32[]{:S(2)}, u32[]{:S(2)}) collective-permute-start(f32[5,3,4,128]{3,2,1,0:T(4,128)S(1)} %slice.110), channel_id=1, source_target_pairs={{0,2},{1,3},{2,0},{3,1},{4,6},{5,7},{6,4},{7,5},{8,10},{9,11},{10,... | collective-permute-start | bytes 92168 | tf_op jit(solution)/shard_map/ppermute | solution.py:110
  12.8 0.2 collective-permute-start.7
  12.9 3.6 %collective-permute-start.5 = (f32[2,15,512]{2,1,0:T(8,128)S(1)}, f32[2,15,512]{2,1,0:T(8,128)S(1)}, u32[]{:S(2)}, u32[]{:S(2)}) collective-permute-start(f32[2,15,512]{2,1,0:T(8,128)S(1)} %get-tuple-element.7), channel_id=1, source_target_pairs={{0,24},{4,28},{8,0},{12,4},{16,8},{20,12},{24,16},{28,20},{1,25},{... | collective-permute-start | bytes 184328 | tf_op jit(solution)/shard_map/ppermute | solution.py:110
  16.5 0.4 collective-permute-start.4
  16.9 0.1 copy.13.metric_ref
  17.0 3.6 %collective-permute-start.3 = (f32[2,15,512]{2,1,0:T(8,128)S(1)}, f32[2,15,512]{2,1,0:T(8,128)S(1)}, u32[]{:S(2)}, u32[]{:S(2)}) collective-permute-start(f32[2,15,512]{2,1,0:T(8,128)S(1)} %get-tuple-element.7), channel_id=1, source_target_pairs={{0,16},{4,20},{8,24},{12,28},{16,0},{20,4},{24,8},{28,12},{1,17},{... | collective-permute-start | bytes 184328 | tf_op jit(solution)/shard_map/ppermute | solution.py:110
  20.6 0.0 collective-permute-start.2
  20.6 1.0 %collective-permute-start.1 = (f32[2,15,512]{2,1,0:T(8,128)S(1)}, f32[2,15,512]{2,1,0:T(8,128)S(1)}, u32[]{:S(2)}, u32[]{:S(2)}) collective-permute-start(f32[2,15,512]{2,1,0:T(8,128)S(1)} %get-tuple-element.7), channel_id=1, source_target_pairs={{0,8},{4,12},{8,16},{12,20},{16,24},{20,28},{24,0},{28,4},{1,9},{5... | collective-permute-start | bytes 184328 | tf_op jit(solution)/shard_map/ppermute | solution.py:110
  21.6 0.1 slice_add_fusion.3
  21.6 0.1 stack.15.edge_ref
  21.7 1.5 %collective-permute-start = (f32[3,15,512]{2,1,0:T(8,128)S(1)}, f32[3,15,512]{2,1,0:T(8,128)S(1)}, u32[]{:S(2)}, u32[]{:S(2)}) collective-permute-start(f32[3,15,512]{2,1,0:T(8,128)S(1)} %get-tuple-element.6), channel_id=1, source_target_pairs={{0,4},{4,8},{8,12},{12,16},{16,20},{20,24},{24,28},{28,0},{1,5},{5... | collective-permute-start | bytes 276488 | tf_op jit(solution)/shard_map/ppermute | solution.py:110
  23.3 5.2 %collective-permute-start.6 = (f32[3,15,512]{2,1,0:T(8,128)S(1)}, f32[3,15,512]{2,1,0:T(8,128)S(1)}, u32[]{:S(2)}, u32[]{:S(2)}) collective-permute-start(f32[3,15,512]{2,1,0:T(8,128)S(1)} %get-tuple-element.8), channel_id=1, source_target_pairs={{0,28},{4,0},{8,4},{12,8},{16,12},{20,16},{24,20},{28,24},{1,29},{... | collective-permute-start | bytes 276488 | tf_op jit(solution)/shard_map/ppermute | solution.py:110
  28.5 0.0 copy-start.1
  28.5 2.1 %copy-done.1 = f32[5,3,128,512]{3,2,1,0:T(8,128)S(1)} copy-done((f32[5,3,128,512]{3,2,1,0:T(8,128)S(1)}, f32[5,3,128,512]{3,2,1,0:T(8,128)}, u32[]{:S(2)}) %copy-start.1) | copy-done | bytes 3932184
  30.6 5.7 %shard_map.124 = f32[5,3,128,512]{3,2,1,0:T(8,128)} custom-call(f32[5,3,128,512]{3,2,1,0:T(8,128)S(1)} %copy-done.1, f32[5,3,8,128]{3,2,1,0:T(8,128)S(1)} %stack.15.edge_ref, bf16[512,512]{1,0:T(8,128)(2,1)S(1)} %copy-done.9, bf16[512,512]{1,0:T(8,128)(2,1)S(1)} %copy-done.8, f32[8,512]{1,0:T(8,128)S(1)} %copy-done.10, f32[1,512]{1,0:T(1,128)S(1)} %bitcast.2), custom_call_target="tpu_custom_call" | custom-call | flops 3019898880 | bytes 7864320 | tf_op jit(solution)/shard_map/pallas_call | solution.py:163
  36.3 0.1 fusion.23
  36.4 4.2 %shard_map.123 = f32[5,3,128,512]{3,2,1,0:T(8,128)} custom-call(f32[5,3,128,512]{3,2,1,0:T(8,128)S(1)} %copy-done.1, f32[4,15,512]{2,1,0:T(8,128)S(1)} %pad_maximum_fusion.edge_ref, bf16[128,128]{1,0:T(8,128)(2,1)S(1)} %copy-done.4, bf16[128,128]{1,0:T(8,128)(2,1)S(1)} %copy-done.3, f32[128,8]{1,0:T(8,128)S(1)} %copy-done.2, f32[128,1]{1,0:T(8,128)S(1)} %copy.13.metric_ref), custom_call_target="tpu_custom_call" | custom-call | flops 754974720 | bytes 7864320 | tf_op jit(solution)/shard_map/pallas_call | solution.py:193
  (30 shorter events, 0.1 us)
Async XLA Ops:
  0.6 2.1 %copy-start = (f32[5,3,128,512]{3,2,1,0:T(8,128)S(1)}, f32[5,3,128,512]{3,2,1,0:T(8,128)}, u32[]{:S(2)}) copy-start(f32[5,3,128,512]{3,2,1,0:T(8,128)} %u_ref.5) | copy-start | bytes 11796484
  2.7 0.7 %copy-start.5 = (f32[8,512]{1,0:T(8,128)S(1)}, f32[8,512]{1,0:T(8,128)}, u32[]{:S(2)}) copy-start(f32[8,512]{1,0:T(8,128)} %constant.22.clone.wy_ref) | copy-start | bytes 49156
  3.5 0.7 %copy-start.6 = (f32[8,128]{1,0:T(8,128)S(1)}, f32[8,128]{1,0:T(8,128)}, u32[]{:S(2)}) copy-start(f32[8,128]{1,0:T(8,128)} %constant.9.clone.wx_ref) | copy-start | bytes 12292
  4.2 12.7 %copy-start.11 = (f32[128]{0:T(128)S(1)}, f32[128]{0:T(128)}, u32[]{:S(2)}) copy-start(f32[128]{0:T(128)} %param.12) | copy-start | bytes 1540
  4.2 24.4 %copy-start.7 = (f32[512]{0:T(512)S(1)}, f32[512]{0:T(512)}, u32[]{:S(2)}) copy-start(f32[512]{0:T(512)} %param.13) | copy-start | bytes 6148
  4.2 24.4 %copy-start.8 = (bf16[512,512]{1,0:T(8,128)(2,1)S(1)}, bf16[512,512]{1,0:T(8,128)(2,1)}, u32[]{:S(2)}) copy-start(bf16[512,512]{1,0:T(8,128)(2,1)} %constant.24.clone.low_ref) | copy-start | bytes 1572868
  4.2 24.4 %copy-start.9 = (bf16[512,512]{1,0:T(8,128)(2,1)S(1)}, bf16[512,512]{1,0:T(8,128)(2,1)}, u32[]{:S(2)}) copy-start(bf16[512,512]{1,0:T(8,128)(2,1)} %constant.23.clone.high_ref) | copy-start | bytes 1572868
  4.2 24.3 %copy-start.10 = (f32[8,512]{1,0:T(8,128)S(1)}, f32[8,512]{1,0:T(8,128)}, u32[]{:S(2)}) copy-start(f32[8,512]{1,0:T(8,128)} %constant.25.clone.profile_ref) | copy-start | bytes 49156
  9.7 7.3 %collective-permute-start.9 = (f32[5,3,4,128]{3,2,1,0:T(4,128)S(1)}, f32[5,3,4,128]{3,2,1,0:T(4,128)S(1)}, u32[]{:S(2)}, u32[]{:S(2)}) collective-permute-start(f32[5,3,4,128]{3,2,1,0:T(4,128)S(1)} %slice.110), channel_id=1, source_target_pairs={{0,3},{1,0},{2,1},{3,2},{4,7},{5,4},{6,5},{7,6},{8,11},{9,8},{10,9... | collective-permute-start | bytes 92168 | tf_op jit(solution)/shard_map/ppermute | solution.py:110
  12.1 8.4 %collective-permute-start.8 = (f32[5,3,4,128]{3,2,1,0:T(4,128)S(1)}, f32[5,3,4,128]{3,2,1,0:T(4,128)S(1)}, u32[]{:S(2)}, u32[]{:S(2)}) collective-permute-start(f32[5,3,4,128]{3,2,1,0:T(4,128)S(1)} %slice.110), channel_id=1, source_target_pairs={{0,2},{1,3},{2,0},{3,1},{4,6},{5,7},{6,4},{7,5},{8,10},{9,11},{10,... | collective-permute-start | bytes 92168 | tf_op jit(solution)/shard_map/ppermute | solution.py:110
  12.8 7.8 %collective-permute-start.7 = (f32[5,3,4,128]{3,2,1,0:T(4,128)S(1)}, f32[5,3,4,128]{3,2,1,0:T(4,128)S(1)}, u32[]{:S(2)}, u32[]{:S(2)}) collective-permute-start(f32[5,3,4,128]{3,2,1,0:T(4,128)S(1)} %slice.110), channel_id=1, source_target_pairs={{0,1},{1,2},{2,3},{3,0},{4,5},{5,6},{6,7},{7,4},{8,9},{9,10},{10,1... | collective-permute-start | bytes 92168 | tf_op jit(solution)/shard_map/ppermute | solution.py:110
  12.9 8.8 %collective-permute-start.5 = (f32[2,15,512]{2,1,0:T(8,128)S(1)}, f32[2,15,512]{2,1,0:T(8,128)S(1)}, u32[]{:S(2)}, u32[]{:S(2)}) collective-permute-start(f32[2,15,512]{2,1,0:T(8,128)S(1)} %get-tuple-element.7), channel_id=1, source_target_pairs={{0,24},{4,28},{8,0},{12,4},{16,8},{20,12},{24,16},{28,20},{1,25},{... | collective-permute-start | bytes 184328 | tf_op jit(solution)/shard_map/ppermute | solution.py:110
  16.5 6.7 %collective-permute-start.4 = (f32[2,15,512]{2,1,0:T(8,128)S(1)}, f32[2,15,512]{2,1,0:T(8,128)S(1)}, u32[]{:S(2)}, u32[]{:S(2)}) collective-permute-start(f32[2,15,512]{2,1,0:T(8,128)S(1)} %get-tuple-element.7), channel_id=1, source_target_pairs={{0,20},{4,24},{8,28},{12,0},{16,4},{20,8},{24,12},{28,16},{1,21},{... | collective-permute-start | bytes 184328 | tf_op jit(solution)/shard_map/ppermute | solution.py:110
  17.0 19.3 %collective-permute-start.3 = (f32[2,15,512]{2,1,0:T(8,128)S(1)}, f32[2,15,512]{2,1,0:T(8,128)S(1)}, u32[]{:S(2)}, u32[]{:S(2)}) collective-permute-start(f32[2,15,512]{2,1,0:T(8,128)S(1)} %get-tuple-element.7), channel_id=1, source_target_pairs={{0,16},{4,20},{8,24},{12,28},{16,0},{20,4},{24,8},{28,12},{1,17},{... | collective-permute-start | bytes 184328 | tf_op jit(solution)/shard_map/ppermute | solution.py:110
  20.6 15.7 %collective-permute-start.2 = (f32[2,15,512]{2,1,0:T(8,128)S(1)}, f32[2,15,512]{2,1,0:T(8,128)S(1)}, u32[]{:S(2)}, u32[]{:S(2)}) collective-permute-start(f32[2,15,512]{2,1,0:T(8,128)S(1)} %get-tuple-element.7), channel_id=1, source_target_pairs={{0,12},{4,16},{8,20},{12,24},{16,28},{20,0},{24,4},{28,8},{1,13},{... | collective-permute-start | bytes 184328 | tf_op jit(solution)/shard_map/ppermute | solution.py:110
  20.6 15.7 %collective-permute-start.1 = (f32[2,15,512]{2,1,0:T(8,128)S(1)}, f32[2,15,512]{2,1,0:T(8,128)S(1)}, u32[]{:S(2)}, u32[]{:S(2)}) collective-permute-start(f32[2,15,512]{2,1,0:T(8,128)S(1)} %get-tuple-element.7), channel_id=1, source_target_pairs={{0,8},{4,12},{8,16},{12,20},{16,24},{20,28},{24,0},{28,4},{1,9},{5... | collective-permute-start | bytes 184328 | tf_op jit(solution)/shard_map/ppermute | solution.py:110
  21.7 14.6 %collective-permute-start = (f32[3,15,512]{2,1,0:T(8,128)S(1)}, f32[3,15,512]{2,1,0:T(8,128)S(1)}, u32[]{:S(2)}, u32[]{:S(2)}) collective-permute-start(f32[3,15,512]{2,1,0:T(8,128)S(1)} %get-tuple-element.6), channel_id=1, source_target_pairs={{0,4},{4,8},{8,12},{12,16},{16,20},{20,24},{24,28},{28,0},{1,5},{5... | collective-permute-start | bytes 276488 | tf_op jit(solution)/shard_map/ppermute | solution.py:110
  23.3 13.1 %collective-permute-start.6 = (f32[3,15,512]{2,1,0:T(8,128)S(1)}, f32[3,15,512]{2,1,0:T(8,128)S(1)}, u32[]{:S(2)}, u32[]{:S(2)}) collective-permute-start(f32[3,15,512]{2,1,0:T(8,128)S(1)} %get-tuple-element.8), channel_id=1, source_target_pairs={{0,28},{4,0},{8,4},{12,8},{16,12},{20,16},{24,20},{28,24},{1,29},{... | collective-permute-start | bytes 276488 | tf_op jit(solution)/shard_map/ppermute | solution.py:110
  28.5 2.1 %copy-start.1 = (f32[5,3,128,512]{3,2,1,0:T(8,128)S(1)}, f32[5,3,128,512]{3,2,1,0:T(8,128)}, u32[]{:S(2)}) copy-start(f32[5,3,128,512]{3,2,1,0:T(8,128)} %u_ref.5) | copy-start | bytes 11796484
  30.6 5.8 %copy-start.2 = (f32[128,8]{1,0:T(8,128)S(1)}, f32[128,8]{1,0:T(8,128)}, u32[]{:S(2)}) copy-start(f32[128,8]{1,0:T(8,128)} %constant.28.clone.profile_ref) | copy-start | bytes 12292
  30.6 5.8 %copy-start.3 = (bf16[128,128]{1,0:T(8,128)(2,1)S(1)}, bf16[128,128]{1,0:T(8,128)(2,1)}, u32[]{:S(2)}) copy-start(bf16[128,128]{1,0:T(8,128)(2,1)} %constant.27.clone.low_ref) | copy-start | bytes 98308
  30.6 5.8 %copy-start.4 = (bf16[128,128]{1,0:T(8,128)(2,1)S(1)}, bf16[128,128]{1,0:T(8,128)(2,1)}, u32[]{:S(2)}) copy-start(bf16[128,128]{1,0:T(8,128)(2,1)} %constant.26.clone.high_ref) | copy-start | bytes 98308

commit v2 on v1

v2 whole, which is shorter than its diff:
```python
import jax
import jax.numpy as jnp
import ml_dtypes
import numpy as np
from jax import lax
from jax.experimental import pallas as pl
from jax.experimental.pallas import tpu as pltpu
from jax.sharding import PartitionSpec as P

ALPHA = 0.47
HALF_A = (ALPHA + 2.0) / 3.0
QUARTER_B = (4.0 * ALPHA - 1.0) / 12.0

ROOT = (-1.0 + np.sqrt(1.0 - 4.0 * ALPHA * ALPHA)) / (2.0 * ALPHA)
GAIN = 1.0 / (1.0 + 2.0 * ALPHA * ROOT)
KAPPA = GAIN * (HALF_A * (ROOT - 1.0 / ROOT) + QUARTER_B * (ROOT**2 - ROOT**-2))
DELTA = GAIN * QUARTER_B * (1.0 / ROOT - ROOT)

MIB = 1 << 20


def piece_matrix(extent):
    place = np.arange(extent)
    gap = place[:, None] - place[None, :]
    size = np.abs(gap)
    whole = np.sign(gap) * (KAPPA * ROOT**size + np.where(size == 1, DELTA, 0.0))
    high = whole.astype(ml_dtypes.bfloat16)
    low = (whole - high.astype(np.float64)).astype(ml_dtypes.bfloat16)
    return high, low


def sum_weights(extent):
    place = np.arange(extent)
    return np.stack([ROOT ** (extent - place), ROOT ** (place + 1)]).astype(np.float32)


def edge_profiles(extent, members):
    place = np.arange(extent)
    whole_turn = 1.0 - ROOT ** (extent * members)
    rows = np.zeros((8, extent))
    rows[0] = KAPPA * ROOT**place / whole_turn
    rows[1] = -KAPPA * ROOT ** (extent - 1 - place) / whole_turn
    rows[2, 0] = DELTA
    rows[3, -1] = -DELTA
    return rows.astype(np.float32)


def split(values):
    high = values.astype(jnp.bfloat16)
    return high, (values - high.astype(jnp.float32)).astype(jnp.bfloat16)


def dot(left, right):
    return jnp.dot(left, right, preferred_element_type=jnp.float32)


LAST, UP, DOWN, FIRST = range(4)


def partners(axis):
    count = lax.axis_size(axis)
    me = lax.axis_index(axis)
    return [(q, {axis: lax.rem(me + q, count)}) for q in range(1, count)]


def reach(own, arrived, factor):
    count = arrived.shape[0]
    below, above = own[UP], own[DOWN]
    for q in range(count - 1, 0, -1):
        below = arrived[q, UP] + factor * below
        above = arrived[count - q, DOWN] + factor * above
    return below, above, arrived[1, LAST], arrived[count - 1, FIRST]


def solve_kernel(
    u_ref, wx_ref, wy_ref, xh_ref, xl_ref, yh_ref, yl_ref,
    first_ref, second_ref, edge_x_ref, edge_y_ref,
    own_x, own_y, far_x, far_y, send_x, got_x, send_y, got_y,
):
    slabs, rows, columns = u_ref.shape
    padded = own_x.shape[1]
    along_x, along_y = partners("gx"), partners("gy")
    mesh_id = pl.DeviceIdType.MESH

    barrier = pltpu.get_barrier_semaphore()
    for _, device in along_x + along_y:
        pl.semaphore_signal(barrier, inc=1, device_id=device, device_id_type=mesh_id)

    own_x[...] = jnp.zeros_like(own_x)
    lane = lax.broadcasted_iota(jnp.int32, (rows, 128), 1)

    def sums(slab, gathered):
        u = u_ref[slab]
        own_x[LAST, pl.ds(slab, 1), :] = u[rows - 1 :]
        own_x[UP, pl.ds(slab, 1), :] = jnp.sum(u * wx_ref[:, 0:1], axis=0, keepdims=True)
        own_x[DOWN, pl.ds(slab, 1), :] = jnp.sum(u * wx_ref[:, 1:2], axis=0, keepdims=True)
        own_x[FIRST, pl.ds(slab, 1), :] = u[0:1]
        ends = (
            u[:, columns - 1 :],
            jnp.sum(u * wy_ref[0:1, :], axis=1, keepdims=True),
            jnp.sum(u * wy_ref[1:2, :], axis=1, keepdims=True),
            u[:, 0:1],
        )
        for k in range(4):
            gathered = jnp.where(lane == k * padded + slab, ends[k], gathered)
        return gathered

    gathered = lax.fori_loop(0, slabs, sums, jnp.zeros((rows, 128), jnp.float32)).T
    for k in range(4):
        own_y[k] = gathered[k * padded : (k + 1) * padded]

    pl.semaphore_wait(barrier, len(along_x) + len(along_y))
    copies = []
    for q, device in along_y:
        copies.append(pltpu.make_async_remote_copy(
            src_ref=own_y, dst_ref=far_y.at[q], send_sem=send_y.at[q], recv_sem=got_y.at[q],
            device_id=device, device_id_type=mesh_id,
        ))
    for q, device in along_x:
        low = LAST if q == 1 else UP
        high = FIRST if q == len(along_x) else DOWN
        part = pl.ds(low, high - low + 1)
        copies.append(pltpu.make_async_remote_copy(
            src_ref=own_x.at[part], dst_ref=far_x.at[q, part],
            send_sem=send_x.at[q], recv_sem=got_x.at[q],
            device_id=device, device_id_type=mesh_id,
        ))
    for copy in copies:
        copy.start()

    group = 3 if slabs % 3 == 0 else 1

    def multiply(step, carry):
        wide = jnp.concatenate([xh_ref[...], xh_ref[...], xl_ref[...]], axis=1)
        u = u_ref[pl.ds(step * group, group)]
        u_high, u_low = split(u)
        flat_high = u_high.reshape(group * rows, columns)
        flat_low = u_low.reshape(group * rows, columns)
        total = dot(flat_high, yh_ref[...]) + dot(flat_low, yh_ref[...]) + dot(flat_high, yl_ref[...])
        second_ref[pl.ds(step * group, group)] = total.reshape(group, rows, columns)
        for k in range(group):
            stack = jnp.concatenate([u_high[k], u_low[k], u_high[k]], axis=0)
            first_ref[step * group + k] = dot(wide, stack)
        return carry

    lax.fori_loop(0, slabs // group, multiply, 0)

    for copy in copies:
        copy.wait()
    for out, own, far, extent in (
        (edge_x_ref, own_x, far_x, rows), (edge_y_ref, own_y, far_y, columns),
    ):
        for k, values in enumerate(reach(own, far, np.float32(ROOT**extent))):
            out[k] = values


def finish_kernel(
    first_ref, second_ref, edge_x_ref, edge_y_ref, px_ref, py_ref, mx_ref, my_ref,
    slope_x_ref, slope_y_ref,
):
    planes = first_ref.shape[0]
    step = pl.program_id(0)
    for plane in range(planes):
        slab = step * planes + plane
        total = first_ref[plane]
        for k in range(4):
            total = total + px_ref[:, k : k + 1] * edge_x_ref[k, pl.ds(slab, 1), :]
        slope_x_ref[0, plane] = total * mx_ref[...]
        edges = [edge_y_ref[k, pl.ds(slab, 1), :] for k in range(4)]
        edge = jnp.concatenate(edges + edges, axis=0).T
        total = second_ref[plane]
        for k in range(4):
            total = total + edge[:, k : k + 1] * py_ref[k : k + 1, :]
        slope_y_ref[0, plane] = total * my_ref[...]


def whole(shape):
    return pl.BlockSpec(shape, lambda f: (0,) * len(shape))


def shards(fields, metric_first, metric_second):
    count, planes, rows, columns = fields.shape
    slabs = count * planes
    padded = -(-slabs // 8) * 8
    gx, gy = lax.axis_size("gx"), lax.axis_size("gy")
    size = fields.size
    f32 = jnp.float32
    shape = jax.ShapeDtypeStruct
    in_vmem = pl.BlockSpec(memory_space=pltpu.VMEM)

    x_high, x_low = piece_matrix(rows)
    y_high, y_low = (np.ascontiguousarray(part.T) for part in piece_matrix(columns))
    total_first, total_second, edge_x, edge_y = pl.pallas_call(
        solve_kernel,
        in_specs=[in_vmem] * 7,
        out_specs=[in_vmem] * 4,
        out_shape=[
            shape((slabs, rows, columns), f32),
            shape((slabs, rows, columns), f32),
            shape((4, padded, columns), f32),
            shape((4, padded, rows), f32),
        ],
        scratch_shapes=[
            pltpu.VMEM((4, padded, columns), f32),
            pltpu.VMEM((4, padded, rows), f32),
            pltpu.VMEM((gx, 4, padded, columns), f32),
            pltpu.VMEM((gy, 4, padded, rows), f32),
            pltpu.SemaphoreType.DMA((gx,)),
            pltpu.SemaphoreType.DMA((gx,)),
            pltpu.SemaphoreType.DMA((gy,)),
            pltpu.SemaphoreType.DMA((gy,)),
        ],
        compiler_params=pltpu.CompilerParams(
            collective_id=0, has_side_effects=True, vmem_limit_bytes=40 * MIB
        ),
        cost_estimate=pl.CostEstimate(
            flops=6 * size * (rows + columns), bytes_accessed=4 * size, transcendentals=0
        ),
    )(
        fields.reshape(slabs, rows, columns),
        np.ascontiguousarray(sum_weights(rows).T), sum_weights(columns),
        x_high, x_low, y_high, y_low,
    )

    total_spec = pl.BlockSpec((planes, rows, columns), lambda f: (f, 0, 0))
    slope_spec = pl.BlockSpec((1, planes, rows, columns), lambda f: (f, 0, 0, 0))
    return pl.pallas_call(
        finish_kernel,
        grid=(count,),
        in_specs=[
            total_spec,
            total_spec,
            whole((4, padded, columns)),
            whole((4, padded, rows)),
            whole((rows, 8)),
            whole((8, columns)),
            whole((rows, 1)),
            whole((1, columns)),
        ],
        out_specs=[slope_spec, slope_spec],
        out_shape=[shape(fields.shape, f32)] * 2,
        compiler_params=pltpu.CompilerParams(vmem_limit_bytes=24 * MIB),
        cost_estimate=pl.CostEstimate(flops=20 * size, bytes_accessed=16 * size, transcendentals=0),
    )(
        total_first, total_second, edge_x, edge_y,
        np.ascontiguousarray(edge_profiles(rows, gx).T), edge_profiles(columns, gy),
        metric_first[:, None], metric_second[None, :],
    )


def solution(mesh):
    placed = (P(None, None, "gx", "gy"), P("gx"), P("gy"))
    return jax.shard_map(
        shards,
        mesh=mesh,
        in_specs=placed,
        out_specs=(P(None, None, "gx", "gy"), P(None, None, "gx", "gy")),
        check_vma=False,
    )
```

time: 40.9 us -> 32.9 us (0.80)
  the two profiles are of different devices: /device:TPU:0 before, /device:TPU:8 now
where the time goes in v2:
time: 32.9 us; the launch traced here: 32.5 us
  Pallas kernels  23.8 us (72%)
  local copies, waits for them, and re-layouts  8 us (24%)
  between operations  0.67 us (2%)
    pallas_call x1, Pallas kernels, shards(): pl.pallas_call(solve_kernel, in_specs=[in_vmem] * 7, out_specs=[in_vmem]...  18 us
    unnamed x20, local copies, waits for them, and re-layouts  7.24 us
    pallas_call x1, Pallas kernels, shards(): pl.pallas_call(finish_kernel, grid=(count,), in_specs=[total_spec, total_...  5.81 us
    broadcast_in_dim x1, local copies, waits for them, and re-layouts, shards(): metric_first[:, None]  0.76 us

profile of v2, /device:TPU:8, one launch (start us, length us, event | category | flops | bytes accessed | tf_op | source)
XLA Modules:
  0.0 32.5 jit_solution(924903541529466461)
XLA Ops:
  0.6 0.8 %copy.13.mx_ref = f32[128,1]{1,0:T(8,128)S(1)} copy(f32[128,1]{0,1:T(1,128)} %bitcast.5) | data formatting | bytes 1024 | tf_op jit(solution)/shard_map/broadcast_in_dim | solution.py:247
  1.4 0.0 copy-start.3
  1.4 2.1 %copy-done.3 = f32[5,3,128,512]{3,2,1,0:T(8,128)S(1)} copy-done((f32[5,3,128,512]{3,2,1,0:T(8,128)S(1)}, f32[5,3,128,512]{3,2,1,0:T(8,128)}, u32[]{:S(2)}) %copy-start.3) | copy-done | bytes 3932184
  3.5 0.0 copy-start.4
  3.5 1.0 %copy-done.4 = bf16[512,512]{1,0:T(8,128)(2,1)S(1)} copy-done((bf16[512,512]{1,0:T(8,128)(2,1)S(1)}, bf16[512,512]{1,0:T(8,128)(2,1)}, u32[]{:S(2)}) %copy-start.4) | copy-done | bytes 524312
  4.5 0.0 copy-start.5
  4.5 1.0 %copy-done.5 = bf16[512,512]{1,0:T(8,128)(2,1)S(1)} copy-done((bf16[512,512]{1,0:T(8,128)(2,1)S(1)}, bf16[512,512]{1,0:T(8,128)(2,1)}, u32[]{:S(2)}) %copy-start.5) | copy-done | bytes 524312
  5.6 0.0 copy-start.6
  5.6 0.8 %copy-done.6 = f32[128,2]{1,0:T(8,128)S(1)} copy-done((f32[128,2]{1,0:T(8,128)S(1)}, f32[128,2]{1,0:T(8,128)}, u32[]{:S(2)}) %copy-start.6) | copy-done | bytes 1048
  6.4 0.0 copy-start.7
  6.4 0.8 %copy-done.7 = bf16[128,128]{1,0:T(8,128)(2,1)S(1)} copy-done((bf16[128,128]{1,0:T(8,128)(2,1)S(1)}, bf16[128,128]{1,0:T(8,128)(2,1)}, u32[]{:S(2)}) %copy-start.7) | copy-done | bytes 32792
  7.2 0.0 copy-start.8
  7.2 0.8 %copy-done.8 = bf16[128,128]{1,0:T(8,128)(2,1)S(1)} copy-done((bf16[128,128]{1,0:T(8,128)(2,1)S(1)}, bf16[128,128]{1,0:T(8,128)(2,1)}, u32[]{:S(2)}) %copy-start.8) | copy-done | bytes 32792
  7.9 0.0 copy-start.9
  7.9 0.7 %copy-done.9 = f32[2,512]{1,0:T(2,128)S(1)} copy-done((f32[2,512]{1,0:T(2,128)S(1)}, f32[2,512]{1,0:T(2,128)}, u32[]{:S(2)}) %copy-start.9) | copy-done | bytes 4120
  8.6 0.0 copy-start
  8.6 0.0 copy-start.1
  8.6 0.0 copy-start.2
  8.6 18.0 %shard_map.122 = (f32[15,128,512]{2,1,0:T(8,128)S(1)}, f32[15,128,512]{2,1,0:T(8,128)S(1)}, f32[4,16,512]{2,1,0:T(8,128)S(1)}, f32[4,16,128]{2,1,0:T(8,128)S(1)}) custom-call(f32[15,128,512]{2,1,0:T(8,128)S(1)} %bitcast.4, f32[128,2]{1,0:T(8,128)S(1)} %copy-done.6, f32[2,512]{1,0:T(2,128)S(1)} %copy-done.9, bf16[128,128]{1,0:T(8,128)(2,1)S(1)} %copy-done.8, ...), custom_call_target="tpu_custom_call" | custom-call | flops 3774873600 | bytes 3932160 | tf_op jit(solution)/shard_map/pallas_call | solution.py:193
  26.6 0.0 copy-done
  26.6 0.0 copy-done.1
  26.6 0.0 copy-done.2
  26.6 5.8 %shard_map.123 = (f32[5,3,128,512]{3,2,1,0:T(8,128)}, f32[5,3,128,512]{3,2,1,0:T(8,128)}) custom-call(f32[15,128,512]{2,1,0:T(8,128)S(1)} %get-tuple-element.6.first_ref, f32[15,128,512]{2,1,0:T(8,128)S(1)} %get-tuple-element.7.second_ref, f32[4,16,512]{2,1,0:T(8,128)S(1)} %get-tuple-element.8.edge_x_ref, f32[4,16,128]{2,1,0:T(8,128)S(1)} %get-tuple-element.9.edge_y_ref, ...), custom_call_target="tpu_custom_call" | custom-call | flops 19660800 | bytes 15728640 | tf_op jit(solution)/shard_map/pallas_call | solution.py:227
Async XLA Ops:
  1.4 2.1 %copy-start.3 = (f32[5,3,128,512]{3,2,1,0:T(8,128)S(1)}, f32[5,3,128,512]{3,2,1,0:T(8,128)}, u32[]{:S(2)}) copy-start(f32[5,3,128,512]{3,2,1,0:T(8,128)} %param.11) | copy-start | bytes 11796484
  3.5 1.0 %copy-start.4 = (bf16[512,512]{1,0:T(8,128)(2,1)S(1)}, bf16[512,512]{1,0:T(8,128)(2,1)}, u32[]{:S(2)}) copy-start(bf16[512,512]{1,0:T(8,128)(2,1)} %constant.21.clone.yl_ref) | copy-start | bytes 1572868
  4.5 1.0 %copy-start.5 = (bf16[512,512]{1,0:T(8,128)(2,1)S(1)}, bf16[512,512]{1,0:T(8,128)(2,1)}, u32[]{:S(2)}) copy-start(bf16[512,512]{1,0:T(8,128)(2,1)} %constant.20.clone.yh_ref) | copy-start | bytes 1572868
  5.6 0.8 %copy-start.6 = (f32[128,2]{1,0:T(8,128)S(1)}, f32[128,2]{1,0:T(8,128)}, u32[]{:S(2)}) copy-start(f32[128,2]{1,0:T(8,128)} %constant.16.clone.wx_ref) | copy-start | bytes 3076
  6.4 0.8 %copy-start.7 = (bf16[128,128]{1,0:T(8,128)(2,1)S(1)}, bf16[128,128]{1,0:T(8,128)(2,1)}, u32[]{:S(2)}) copy-start(bf16[128,128]{1,0:T(8,128)(2,1)} %constant.19.clone.xl_ref) | copy-start | bytes 98308
  7.2 0.8 %copy-start.8 = (bf16[128,128]{1,0:T(8,128)(2,1)S(1)}, bf16[128,128]{1,0:T(8,128)(2,1)}, u32[]{:S(2)}) copy-start(bf16[128,128]{1,0:T(8,128)(2,1)} %constant.18.clone.xh_ref) | copy-start | bytes 98308
  7.9 0.7 %copy-start.9 = (f32[2,512]{1,0:T(2,128)S(1)}, f32[2,512]{1,0:T(2,128)}, u32[]{:S(2)}) copy-start(f32[2,512]{1,0:T(2,128)} %constant.17.clone.wy_ref) | copy-start | bytes 12292
  8.6 18.0 %copy-start = (f32[128,8]{1,0:T(8,128)S(1)}, f32[128,8]{1,0:T(8,128)}, u32[]{:S(2)}) copy-start(f32[128,8]{1,0:T(8,128)} %constant.22.clone.px_ref) | copy-start | bytes 12292
  8.6 18.0 %copy-start.1 = (f32[8,512]{1,0:T(8,128)S(1)}, f32[8,512]{1,0:T(8,128)}, u32[]{:S(2)}) copy-start(f32[8,512]{1,0:T(8,128)} %constant.23.clone.py_ref) | copy-start | bytes 49156
  8.6 18.0 %copy-start.2 = (f32[512]{0:T(512)S(1)}, f32[512]{0:T(512)}, u32[]{:S(2)}) copy-start(f32[512]{0:T(512)} %param.13) | copy-start | bytes 6148

commit v3 on v2

--- a/solution.py
+++ b/solution.py
@@ -1,3 +1,5 @@
+import functools
+
 import jax
 import jax.numpy as jnp
 import ml_dtypes
@@ -32,6 +34,10 @@
 def sum_weights(extent):
     place = np.arange(extent)
     return np.stack([ROOT ** (extent - place), ROOT ** (place + 1)]).astype(np.float32)
+
+
+def over_lanes(rows):
+    return np.ascontiguousarray(np.broadcast_to(rows[:, :, None], rows.shape + (128,)))
 
 
 def edge_profiles(extent, members):
@@ -73,15 +79,34 @@
 
 
 def solve_kernel(
+    group, u_hbm, wx_hbm, wy_hbm, xh_hbm, xl_hbm, yh_hbm, yl_hbm,
+    first_ref, second_ref, edge_x_ref, edge_y_ref,
     u_ref, wx_ref, wy_ref, xh_ref, xl_ref, yh_ref, yl_ref,
-    first_ref, second_ref, edge_x_ref, edge_y_ref,
-    own_x, own_y, far_x, far_y, send_x, got_x, send_y, got_y,
+    own_x, own_y, far_x, far_y, u_sem, load_sem, send_x, got_x, send_y, got_y,
 ):
     slabs, rows, columns = u_ref.shape
     padded = own_x.shape[1]
     along_x, along_y = partners("gx"), partners("gy")
     mesh_id = pl.DeviceIdType.MESH
 
+    def chunk(step):
+        part = pl.ds(step * group, group)
+        return pltpu.make_async_copy(u_hbm.at[part], u_ref.at[part], u_sem.at[step])
+
+    constants = (
+        (wx_hbm, wx_ref), (wy_hbm, wy_ref), (xh_hbm, xh_ref), (xl_hbm, xl_ref),
+        (yh_hbm, yh_ref), (yl_hbm, yl_ref),
+    )
+    loads = [
+        pltpu.make_async_copy(*pair, load_sem.at[k]) for k, pair in enumerate(constants)
+    ]
+    for load in loads[:2]:
+        load.start()
+    for step in range(slabs // group):
+        chunk(step).start()
+    for load in loads[2:]:
+        load.start()
+
     barrier = pltpu.get_barrier_semaphore()
     for _, device in along_x + along_y:
         pl.semaphore_signal(barrier, inc=1, device_id=device, device_id_type=mesh_id)
@@ -90,22 +115,38 @@
     lane = lax.broadcasted_iota(jnp.int32, (rows, 128), 1)
 
     def sums(slab, gathered):
-        u = u_ref[slab]
-        own_x[LAST, pl.ds(slab, 1), :] = u[rows - 1 :]
-        own_x[UP, pl.ds(slab, 1), :] = jnp.sum(u * wx_ref[:, 0:1], axis=0, keepdims=True)
-        own_x[DOWN, pl.ds(slab, 1), :] = jnp.sum(u * wx_ref[:, 1:2], axis=0, keepdims=True)
-        own_x[FIRST, pl.ds(slab, 1), :] = u[0:1]
+        own_x[LAST, pl.ds(slab, 1), :] = u_ref[slab, rows - 1 :]
+        own_x[FIRST, pl.ds(slab, 1), :] = u_ref[slab, 0:1]
+        up, down, lines = 0.0, 0.0, ([], [])
+        for at in range(0, columns, 128):
+            u = u_ref[slab, :, at : at + 128]
+            for k in range(2):
+                lines[k].append(jnp.sum(u * wx_ref[k], axis=0, keepdims=True))
+            up = up + u * wy_ref[0:1, at : at + 128]
+            down = down + u * wy_ref[1:2, at : at + 128]
+        own_x[UP, pl.ds(slab, 1), :] = jnp.concatenate(lines[0], axis=1)
+        own_x[DOWN, pl.ds(slab, 1), :] = jnp.concatenate(lines[1], axis=1)
         ends = (
-            u[:, columns - 1 :],
-            jnp.sum(u * wy_ref[0:1, :], axis=1, keepdims=True),
-            jnp.sum(u * wy_ref[1:2, :], axis=1, keepdims=True),
-            u[:, 0:1],
+            u_ref[slab, :, columns - 128 :][:, 127:],
+            jnp.sum(up, axis=1, keepdims=True),
+            jnp.sum(down, axis=1, keepdims=True),
+            u_ref[slab, :, :128][:, 0:1],
         )
         for k in range(4):
             gathered = jnp.where(lane == k * padded + slab, ends[k], gathered)
         return gathered
 
-    gathered = lax.fori_loop(0, slabs, sums, jnp.zeros((rows, 128), jnp.float32)).T
+    def sums_of_chunk(step, gathered):
+        chunk(step).wait()
+        for k in range(group):
+            gathered = sums(step * group + k, gathered)
+        return gathered
+
+    for load in loads[:2]:
+        load.wait()
+    gathered = lax.fori_loop(
+        0, slabs // group, sums_of_chunk, jnp.zeros((rows, 128), jnp.float32)
+    ).T
     for k in range(4):
         own_y[k] = gathered[k * padded : (k + 1) * padded]
 
@@ -128,7 +169,8 @@
     for copy in copies:
         copy.start()
 
-    group = 3 if slabs % 3 == 0 else 1
+    for load in loads[2:]:
+        load.wait()
 
     def multiply(step, carry):
         wide = jnp.concatenate([xh_ref[...], xh_ref[...], xl_ref[...]], axis=1)
@@ -155,27 +197,56 @@
 
 
 def finish_kernel(
-    first_ref, second_ref, edge_x_ref, edge_y_ref, px_ref, py_ref, mx_ref, my_ref,
-    slope_x_ref, slope_y_ref,
+    group, first_ref, second_ref, edge_x_ref, edge_y_ref, px_ref, py_ref, mx_ref, my_ref,
+    x_hbm, y_hbm, x_ref, y_ref, x_sem, y_sem,
 ):
-    planes = first_ref.shape[0]
-    step = pl.program_id(0)
-    for plane in range(planes):
-        slab = step * planes + plane
-        total = first_ref[plane]
-        for k in range(4):
-            total = total + px_ref[:, k : k + 1] * edge_x_ref[k, pl.ds(slab, 1), :]
-        slope_x_ref[0, plane] = total * mx_ref[...]
-        edges = [edge_y_ref[k, pl.ds(slab, 1), :] for k in range(4)]
-        edge = jnp.concatenate(edges + edges, axis=0).T
-        total = second_ref[plane]
-        for k in range(4):
-            total = total + edge[:, k : k + 1] * py_ref[k : k + 1, :]
-        slope_y_ref[0, plane] = total * my_ref[...]
-
-
-def whole(shape):
-    return pl.BlockSpec(shape, lambda f: (0,) * len(shape))
+    slabs, rows, columns = first_ref.shape
+    metric_column = jnp.broadcast_to(mx_ref[...], (8, rows)).T[:, 0:1]
+    metric_wide = jnp.broadcast_to(metric_column, (rows, 128))
+
+    def outward(step):
+        part = pl.ds(step * group, group)
+        return (
+            pltpu.make_async_copy(x_ref.at[part], x_hbm.at[part], x_sem.at[step]),
+            pltpu.make_async_copy(y_ref.at[part], y_hbm.at[part], y_sem.at[step]),
+        )
+
+    def finish(step, carry):
+        to_x, to_y = outward(step)
+        for k in range(group):
+            slab = step * group + k
+            edges = [edge_x_ref[k, pl.ds(slab, 1), :] for k in range(4)]
+            for at in range(0, columns, 128):
+                tile = slice(at, at + 128)
+                total = first_ref[slab, :, tile]
+                total = total + px_ref[0] * edges[0][:, tile] + px_ref[1] * edges[1][:, tile]
+                x_ref[slab, :, tile] = total * metric_wide
+            for row, value in ((0, DELTA * edges[2]), (rows - 1, -DELTA * edges[3])):
+                at = pl.ds(row, 1)
+                x_ref[slab, at, :] = x_ref[slab, at, :] + value * metric_column[row : row + 1]
+        to_x.start()
+        for k in range(group):
+            slab = step * group + k
+            edges = [edge_y_ref[k, pl.ds(slab, 1), :] for k in range(4)]
+            edge = jnp.concatenate(edges + edges, axis=0).T
+            for at in range(0, columns, 128):
+                tile = slice(at, at + 128)
+                total = second_ref[slab, :, tile]
+                terms = [0, 1] + [2] * (at == 0) + [3] * (at == columns - 128)
+                for k in terms:
+                    total = total + edge[:, k : k + 1] * py_ref[k : k + 1, tile]
+                y_ref[slab, :, tile] = total * my_ref[:, tile]
+        to_y.start()
+        return carry
+
+    lax.fori_loop(0, slabs // group, finish, 0)
+
+    def drain(step, carry):
+        for copy in outward(step):
+            copy.wait()
+        return carry
+
+    lax.fori_loop(0, slabs // group, drain, 0)
 
 
 def shards(fields, metric_first, metric_second):
@@ -188,23 +259,33 @@
     shape = jax.ShapeDtypeStruct
     in_vmem = pl.BlockSpec(memory_space=pltpu.VMEM)
 
+    in_hbm = pl.BlockSpec(memory_space=pltpu.HBM)
+    slab_shape = (slabs, rows, columns)
+
     x_high, x_low = piece_matrix(rows)
     y_high, y_low = (np.ascontiguousarray(part.T) for part in piece_matrix(columns))
+    loaded = (
+        over_lanes(sum_weights(rows)), sum_weights(columns), x_high, x_low, y_high, y_low
+    )
     total_first, total_second, edge_x, edge_y = pl.pallas_call(
-        solve_kernel,
-        in_specs=[in_vmem] * 7,
+        functools.partial(solve_kernel, planes),
+        in_specs=[in_hbm] * 7,
         out_specs=[in_vmem] * 4,
         out_shape=[
-            shape((slabs, rows, columns), f32),
-            shape((slabs, rows, columns), f32),
+            shape(slab_shape, f32),
+            shape(slab_shape, f32),
             shape((4, padded, columns), f32),
             shape((4, padded, rows), f32),
         ],
-        scratch_shapes=[
+        scratch_shapes=[pltpu.VMEM(slab_shape, f32)]
+        + [pltpu.VMEM(part.shape, part.dtype) for part in loaded]
+        + [
             pltpu.VMEM((4, padded, columns), f32),
             pltpu.VMEM((4, padded, rows), f32),
             pltpu.VMEM((gx, 4, padded, columns), f32),
             pltpu.VMEM((gy, 4, padded, rows), f32),
+            pltpu.SemaphoreType.DMA((count,)),
+            pltpu.SemaphoreType.DMA((len(loaded),)),
             pltpu.SemaphoreType.DMA((gx,)),
             pltpu.SemaphoreType.DMA((gx,)),
             pltpu.SemaphoreType.DMA((gy,)),
@@ -216,36 +297,30 @@
         cost_estimate=pl.CostEstimate(
             flops=6 * size * (rows + columns), bytes_accessed=4 * size, transcendentals=0
         ),
-    )(
-        fields.reshape(slabs, rows, columns),
-        np.ascontiguousarray(sum_weights(rows).T), sum_weights(columns),
-        x_high, x_low, y_high, y_low,
-    )
-
-    total_spec = pl.BlockSpec((planes, rows, columns), lambda f: (f, 0, 0))
-    slope_spec = pl.BlockSpec((1, planes, rows, columns), lambda f: (f, 0, 0, 0))
-    return pl.pallas_call(
-        finish_kernel,
-        grid=(count,),
-        in_specs=[
-            total_spec,
-            total_spec,
-            whole((4, padded, columns)),
-            whole((4, padded, rows)),
-            whole((rows, 8)),
-            whole((8, columns)),
-            whole((rows, 1)),
-            whole((1, columns)),
+    )(*(
+        pltpu.with_memory_space_constraint(part, pltpu.HBM)
+        for part in (fields.reshape(slab_shape), *map(jnp.asarray, loaded))
+    ))
+
+    slope_first, slope_second = pl.pallas_call(
+        functools.partial(finish_kernel, planes),
+        in_specs=[in_vmem] * 8,
+        out_specs=[in_hbm] * 2,
+        out_shape=[shape(slab_shape, f32)] * 2,
+        scratch_shapes=[
+            pltpu.VMEM(slab_shape, f32),
+            pltpu.VMEM(slab_shape, f32),
+            pltpu.SemaphoreType.DMA((count,)),
+            pltpu.SemaphoreType.DMA((count,)),
         ],
-        out_specs=[slope_spec, slope_spec],
-        out_shape=[shape(fields.shape, f32)] * 2,
-        compiler_params=pltpu.CompilerParams(vmem_limit_bytes=24 * MIB),
+        compiler_params=pltpu.CompilerParams(vmem_limit_bytes=36 * MIB),
         cost_estimate=pl.CostEstimate(flops=20 * size, bytes_accessed=16 * size, transcendentals=0),
     )(
         total_first, total_second, edge_x, edge_y,
-        np.ascontiguousarray(edge_profiles(rows, gx).T), edge_profiles(columns, gy),
-        metric_first[:, None], metric_second[None, :],
+        over_lanes(edge_profiles(rows, gx)[:2]), edge_profiles(columns, gy),
+        metric_first[None, :], metric_second[None, :],
     )
+    return slope_first.reshape(fields.shape), slope_second.reshape(fields.shape)
 
 
 def solution(mesh):

time: 32.9 us -> 23.5 us (0.71)
  the two profiles are of different devices: /device:TPU:8 before, /device:TPU:0 now
where the time goes in v3:
time: 23.5 us; the launch traced here: 23.1 us
  Pallas kernels  22.4 us (95%)
  between operations  0.7 us (3%)
    pallas_call x1, Pallas kernels, shards(): pl.pallas_call(functools.partial(solve_kernel, planes), in_specs=[in_hbm]...  18.2 us
    pallas_call x1, Pallas kernels, shards(): pl.pallas_call(functools.partial(finish_kernel, planes), in_specs=[in_vme...  4.16 us

profile of v3, /device:TPU:0, one launch (start us, length us, event | category | flops | bytes accessed | tf_op | source)
XLA Modules:
  0.0 23.1 jit_solution(3303445086896911058)
XLA Ops:
  0.6 0.0 copy-start
  0.6 0.0 copy-start.1
  0.7 0.0 copy-start.2
  0.7 0.0 copy-start.3
  0.7 18.2 %shard_map.122 = (f32[15,128,512]{2,1,0:T(8,128)S(1)}, f32[15,128,512]{2,1,0:T(8,128)S(1)}, f32[4,16,512]{2,1,0:T(8,128)S(1)}, f32[4,16,128]{2,1,0:T(8,128)S(1)}) custom-call(f32[15,128,512]{2,1,0:T(8,128)} %bitcast.7, f32[2,128,128]{2,1,0:T(8,128)} %constant.16.clone.wx_hbm, f32[2,512]{1,0:T(2,128)} %constant.17.clone.wy_hbm, ...), custom_call_target="tpu_custom_call" | custom-call | flops 3774873600 | bytes 3932160 | tf_op jit(solution)/shard_map/pallas_call | solution.py:270
  18.9 0.0 copy-done
  18.9 0.0 copy-done.1
  18.9 0.0 copy-done.2
  18.9 0.0 copy-done.3
  18.9 4.2 %shard_map.123 = (f32[15,128,512]{2,1,0:T(8,128)}, f32[15,128,512]{2,1,0:T(8,128)}) custom-call(f32[15,128,512]{2,1,0:T(8,128)S(1)} %get-tuple-element.8.first_ref, f32[15,128,512]{2,1,0:T(8,128)S(1)} %get-tuple-element.9.second_ref, f32[4,16,512]{2,1,0:T(8,128)S(1)} %get-tuple-element.10.edge_x_ref, f32[4,16,128]{2,1,0:T(8,128)S(1)} %get-tuple-element.11.edge_y_ref, ...), custom_call_target="tpu_custom_call" | custom-call | flops 19660800 | bytes 15728640 | tf_op jit(solution)/shard_map/pallas_call | solution.py:305
Async XLA Ops:
  0.6 18.3 %copy-start = (f32[2,128,128]{2,1,0:T(8,128)S(1)}, f32[2,128,128]{2,1,0:T(8,128)}, u32[]{:S(2)}) copy-start(f32[2,128,128]{2,1,0:T(8,128)} %constant.22.clone.px_ref) | copy-start | bytes 393220
  0.6 18.3 %copy-start.1 = (f32[8,512]{1,0:T(8,128)S(1)}, f32[8,512]{1,0:T(8,128)}, u32[]{:S(2)}) copy-start(f32[8,512]{1,0:T(8,128)} %constant.23.clone.py_ref) | copy-start | bytes 49156
  0.7 18.3 %copy-start.2 = (f32[512]{0:T(512)S(1)}, f32[512]{0:T(512)}, u32[]{:S(2)}) copy-start(f32[512]{0:T(512)} %param.13) | copy-start | bytes 6148
  0.7 18.3 %copy-start.3 = (f32[128]{0:T(128)S(1)}, f32[128]{0:T(128)}, u32[]{:S(2)}) copy-start(f32[128]{0:T(128)} %param.12) | copy-start | bytes 1540
